TPU v7x, 512 devices: a whole 4x4x16 slice. The times are simulated.
512 devices in a mesh: depth: 64 (over y, z), dp: 8 (over x, core).
Axes of the slice: x: 4, y: 4, z: 16, core: 2. Of those that a mesh axis runs over, the one named last changes fastest.
Arguments:
- features: bfloat16 [8, 8, 16, 256], P('dp'), may hold values from -6 to 6
- weights: bfloat16 [128, 3, 3, 256, 256], P('depth'), may hold values from -0.125 to 0.125
- gains: float32 [64, 256], P('depth'), may hold values from 0.75 to 1.25
- cotangent: bfloat16 [8, 8, 16, 256], P('dp'), may hold values from -6 to 6
Outputs:
- starts: bfloat16 [64, 8, 8, 16, 256], P('depth', 'dp')
- adjoints: bfloat16 [64, 8, 8, 16, 256], P('depth', 'dp')
- weight_grads: bfloat16 [128, 3, 3, 256, 256], P('depth', None, None, 'dp')
All inputs are finite; a program needn't handle non-finite values.
Results may differ from a plain program's by a relative error of at most 0.035.
The roundings to bfloat16 on the way count: a program that leaves them out, or rounds other values in their place, can miss the bound.
Values may be sent and summed in bfloat16 or wider, within the bound.
A program may use at most 64 MiB of HBM per device.

v0:
```python
import jax
import jax.numpy as jnp
from jax import lax
from jax.sharding import PartitionSpec as P

step_size = 0.15
dims_spec = ("NHWC", "HWIO", "NHWC")


def prefix(value, axis, combine, identity, reverse):
    count, mine = (lax.axis_size(axis), lax.axis_index(axis))
    everything = jax.tree.map(lambda part: lax.all_gather(part, axis), value)
    start = jax.tree.map(
        lambda part, zero: jnp.broadcast_to(jnp.asarray(zero, part.dtype), part.shape),
        value,
        identity,
    )

    def hop(k, before):
        at = count - 1 - k if reverse else k
        reached = at > mine if reverse else at < mine
        new = combine(before, jax.tree.map(lambda part: part[at], everything))
        return jax.tree.map(lambda a, b: jnp.where(reached, a, b), new, before)

    return lax.fori_loop(0, count, hop, start)


def convolve(inputs, kernel):
    return lax.conv_general_dilated(
        inputs,
        kernel,
        (1, 1),
        "SAME",
        dimension_numbers=dims_spec,
        preferred_element_type=jnp.float32,
    )


def layer_apply(state, kernel):
    active = jnp.maximum(state, 0.0).astype(jnp.bfloat16)
    return state + step_size * convolve(active, kernel)


def block_forward(state, kernels):
    inputs = []
    for layer_index in range(kernels.shape[0]):
        inputs.append(state)
        state = layer_apply(state, kernels[layer_index])
    return (state, inputs)


def kernel_grad(active, scaled):
    height = active.shape[1]
    width = active.shape[2]
    channels = active.shape[3]
    padded = jnp.pad(active, ((0, 0), (1, 1), (1, 1), (0, 0)))
    flat = scaled.reshape(-1, scaled.shape[3])
    result = []
    for offset_a in range(3):
        line = []
        for offset_b in range(3):
            window = padded[
                :, offset_a : offset_a + height, offset_b : offset_b + width, :
            ].reshape(-1, channels)
            line.append(jnp.dot(window.T, flat, preferred_element_type=jnp.float32))
        result.append(jnp.stack(line))
    return jnp.stack(result)


def block_backward(inputs, kernels, cotan, with_weights):
    grads = []
    for layer_index in reversed(range(len(inputs))):
        state = inputs[layer_index]
        kernel = kernels[layer_index]
        scaled = (step_size * cotan).astype(jnp.bfloat16)
        if with_weights:
            active = jnp.maximum(state, 0.0).astype(jnp.bfloat16)
            grads.append(kernel_grad(active, scaled))
        flipped = jnp.swapaxes(kernel[::-1, ::-1], 2, 3)
        spread = convolve(scaled, flipped)
        cotan = cotan + jnp.where(state > 0.0, spread, 0.0)
    return (cotan, grads[::-1])


def compose(earlier, later):
    return (later[0] * earlier[0], later[0] * earlier[1] + later[1])


def forward_prefix(scales, offsets):
    neutral = (jnp.ones_like(scales), jnp.zeros_like(offsets))
    return prefix((scales, offsets), "depth", compose, neutral, False)


def backward_prefix(scales, offsets):
    neutral = (jnp.ones_like(scales), jnp.zeros_like(offsets))
    return prefix((scales, offsets), "depth", compose, neutral, True)


def per_device(features, weights, gains, cotangent):
    start = features.astype(jnp.float32)
    ending = cotangent.astype(jnp.float32)
    scales = gains[0]
    states = start
    linear_inputs = []
    for sweep in range(2):
        finals, inputs = block_forward(states, weights)
        linear_inputs = inputs
        offsets = finals - scales * states
        factor, shifted = forward_prefix(scales, offsets)
        states = factor * start + shifted
    ends = ending
    offsets = jnp.zeros_like(ending)
    for sweep in range(2):
        terms = block_backward(linear_inputs, weights, ends, False)[0]
        offsets = terms - scales * ends
        factor, shifted = backward_prefix(scales, offsets)
        ends = factor * ending + shifted
    adjoints = scales * ends + offsets
    grads = jnp.stack(block_backward(linear_inputs, weights, ends, True)[1])
    summed = lax.psum(grads.astype(jnp.bfloat16), "dp").astype(jnp.float32)
    share = grads.shape[3] // lax.axis_size("dp")
    summed = lax.dynamic_slice_in_dim(summed, lax.axis_index("dp") * share, share, 3)
    return (
        states.astype(jnp.bfloat16)[None],
        adjoints.astype(jnp.bfloat16)[None],
        summed.astype(jnp.bfloat16),
    )


def solution(mesh):
    return jax.shard_map(
        per_device,
        mesh=mesh,
        in_specs=(
            P("dp", None, None, None),
            P("depth", None, None, None, None),
            P("depth", None),
            P("dp", None, None, None),
        ),
        out_specs=(
            P("depth", "dp", None, None, None),
            P("depth", "dp", None, None, None),
            P("depth", None, None, "dp", None),
        ),
        check_vma=False,
    )
```

profile of v0, /device:TPU:1, one launch (start us, length us, event | category | flops | bytes accessed | tf_op | source)
XLA Modules:
  0.0 995.6 jit_solution(1366127368527899786)
XLA Ops:
  7.2 1.0 fusion.211
  8.4 1.7 fusion.43
  11.7 74.5 %all-gather.4 = f32[64,1,256]{2,1,0:T(1,128)S(1)} all-gather(f32[1,1,256]{2,1,0:T(1,128)S(1)} %bitcast.525), channel_id=1, replica_groups=mesh['depth'=64,'dp'=8] {'depth'}, dimensions={0}, use_global_device_ids=true | all-gather | bytes 66560 | tf_op jit(solution)/shard_map/all_gather | solution.py:12
  86.9 79.7 %all-gather.10.cloned.1.call-done = f32[64,8,16,256]{3,2,1,0:T(8,128)} async-done(((f32[1,8,16,256]{3,2,1,0:T(8,128)}), f32[64,8,16,256]{3,2,1,0:T(8,128)}) %all-gather.10.cloned.1.call-update) | async-done | bytes 8388624 | tf_op jit(solution)/shard_map/all_gather | solution.py:12
  166.7 66.8 %while.68 = (s32[]{:T(128)}, f32[256]{0:T(256)S(1)}, f32[1,8,16,256]{3,2,1,0:T(8,128)S(1)}, s32[]{:T(128)}, f32[64,256]{1,0:T(8,128)S(1)}, /*index=5*/f32[64,1,8,16,256]{4,3,2,1,0:T(8,128)}, s32[]{:T(128)}, s32[]{:T(128)}) while((s32[]{:T(128)}, f32[256]{0:T(256)S(1)}, f32[1,8,16,256]{3,2,1,0:T(8,128)S(1)}, s32[]{:T(128)}, ...), condition=%wide.region_1.2_spmd.clone, body=%wide.region_0.1_spmd.clone.sunk | while | flops 131844 | bytes 399475 | solution.py:25
  236.4 151.1 %all-gather.12.cloned.1.call-done = f32[64,8,16,256]{3,2,1,0:T(8,128)} async-done(((f32[1,8,16,256]{3,2,1,0:T(8,128)}), f32[64,8,16,256]{3,2,1,0:T(8,128)}) %all-gather.12.cloned.1.call-update) | async-done | bytes 8388624 | tf_op jit(solution)/shard_map/all_gather | solution.py:12
  387.5 66.8 %while.69 = (s32[]{:T(128)}, f32[256]{0:T(256)S(1)}, f32[1,8,16,256]{3,2,1,0:T(8,128)S(1)}, s32[]{:T(128)}, f32[64,256]{1,0:T(8,128)S(1)}, /*index=5*/f32[64,1,8,16,256]{4,3,2,1,0:T(8,128)}, s32[]{:T(128)}, s32[]{:T(128)}) while((s32[]{:T(128)}, f32[256]{0:T(256)S(1)}, f32[1,8,16,256]{3,2,1,0:T(8,128)S(1)}, s32[]{:T(128)}, ...), condition=%wide.region_3.4_spmd.clone, body=%wide.region_2.3_spmd.clone.sunk | while | flops 131844 | bytes 399475 | solution.py:25
  455.2 151.9 %all-gather.14.cloned.1.call-done = f32[64,8,16,256]{3,2,1,0:T(8,128)} async-done(((f32[1,8,16,256]{3,2,1,0:T(8,128)}), f32[64,8,16,256]{3,2,1,0:T(8,128)}) %all-gather.14.cloned.1.call-update) | async-done | bytes 8388624 | tf_op jit(solution)/shard_map/all_gather | solution.py:12
  607.1 67.6 %while.70 = (s32[]{:T(128)}, f32[256]{0:T(256)S(1)}, f32[1,8,16,256]{3,2,1,0:T(8,128)S(1)}, s32[]{:T(128)}, f32[64,256]{1,0:T(8,128)S(1)}, /*index=5*/f32[64,1,8...) while((s32[]{:T(128)}, f32[256]{0:T(256)S(1)}, ...), condition=%wide.region_5.6_spmd.clone, body=%wide.region_4.5_spmd.clone.sunk | while | flops 131848 | bytes 399537 | solution.py:25
  609.2 1.0 fusion.313
  614.5 1.0 fusion.313
  616.6 1.0 fusion.313
  621.9 1.0 fusion.313
  624.0 1.0 fusion.313
  627.2 1.0 fusion.313
  629.3 1.0 fusion.313
  634.6 1.0 fusion.313
  636.7 1.0 fusion.313
  642.0 1.0 fusion.313
  677.2 151.9 %all-gather.16.cloned.1.call-done = f32[64,8,16,256]{3,2,1,0:T(8,128)} async-done(((f32[1,8,16,256]{3,2,1,0:T(8,128)}), f32[64,8,16,256]{3,2,1,0:T(8,128)}) %all-gather.16.cloned.1.call-update) | async-done | bytes 8388624 | tf_op jit(solution)/shard_map/all_gather | solution.py:12
  829.1 67.6 %while.71 = (s32[]{:T(128)}, f32[256]{0:T(256)S(1)}, f32[1,8,16,256]{3,2,1,0:T(8,128)S(1)}, s32[]{:T(128)}, f32[64,256]{1,0:T(8,128)S(1)}, /*index=5*/f32[64,1,8...) while((s32[]{:T(128)}, f32[256]{0:T(256)S(1)}, ...), condition=%wide.region_7.8_spmd.clone, body=%wide.region_6.7_spmd.clone.sunk | while | flops 131848 | bytes 399537 | solution.py:25
  902.9 1.6 pad_maximum_fusion
  904.5 82.8 %all-reduce.4.cloned.1.call-done = bf16[2,3,3,256,256]{4,3,2,1,0:T(8,128)(2,1)} async-done(((bf16[2,3,3,256,256]{4,3,2,1,0:T(8,128)(2,1)}), bf16[2,3,3,256,256]{4,3,2,1,0:T(8,128)(2,1)}) %all-reduce.4.cloned.1.call-update) | async-done | bytes 2359312 | tf_op jit(solution)/shard_map/psum | solution.py:120
  987.4 1.7 convert_convert_fusion
  (887 shorter events, 263.4 us)
Async XLA Ops:
  7.2 3.2 copy-start.5
  7.2 3.0 copy-start.1
  7.2 3.1 copy-start.4
  7.2 159.5 %all-gather.10.cloned.1.call-start = ((), (), s32[]{:S(2)}) async-start(), calls=%async_computation.1 | async-start | bytes 8519680 | tf_op jit(solution)/shard_map/all_gather | solution.py:12
  10.0 0.8 copy-start.3
  10.2 76.0 %copy-start = (bf16[1,8,16,256]{3,2,1,0:T(8,128)(2,1)S(1)}, bf16[1,8,16,256]{3,2,1,0:T(8,128)(2,1)}, u32[]{:S(2)}) copy-start(bf16[1,8,16,256]{3,2,1,0:T(8,128)(2,1)} %param.15) | copy-start | bytes 196612
  11.6 375.9 %all-gather.12.cloned.1.call-start = ((), (), s32[]{:S(2)}) async-start(), calls=%async_computation.2 | async-start | bytes 8519680 | tf_op jit(solution)/shard_map/all_gather | solution.py:12
  235.6 371.5 %all-gather.14.cloned.1.call-start = ((), (), s32[]{:S(2)}) async-start(), calls=%async_computation.3 | async-start | bytes 8519680 | tf_op jit(solution)/shard_map/all_gather | solution.py:12
  455.2 373.9 %all-gather.16.cloned.1.call-start = ((), (), s32[]{:S(2)}) async-start(), calls=%async_computation.4 | async-start | bytes 8519680 | tf_op jit(solution)/shard_map/all_gather | solution.py:12
  677.2 310.2 %all-reduce.4.cloned.1.call-start = ((), (), s32[]{:S(2)}) async-start(), calls=%async_computation | async-start | bytes 4718592 | tf_op jit(solution)/shard_map/psum | solution.py:120
  896.7 0.9 copy-start.2
Sparse Core Ops, SparseCore 0:
  11.7 154.8 all-gather.9
  235.7 151.7 all-gather.11
  455.3 151.7 all-gather.13
  677.3 151.7 all-gather.15
  904.6 82.6 all-reduce.3
where the time goes:
time: 1000 us; the launch traced here: 996 us
  waiting for transfers between devices  618 us (62%)
  other arithmetic  266 us (27%)
  blocking collectives  74.5 us (7%)
  between operations  14.6 us (1%)
    all_gather x4, waiting for transfers between devices, prefix(): everything = jax.tree.map(lambda part: lax.all_gather(part, axis), value)  535 us
    select_n x512, other arithmetic, hop(): return jax.tree.map(lambda a, b: jnp.where(reached, a, b), new, before)  257 us
    psum x1, waiting for transfers between devices, per_device(): summed = lax.psum(grads.astype(jnp.bfloat16), 'dp').astype(jnp.float32)  82.8 us
    all_gather x1, blocking collectives, prefix(): everything = jax.tree.map(lambda part: lax.all_gather(part, axis), value)  74.5 us
  transfers between devices with their start and end apart: 5, of which 5 were waited for; matrix products, arithmetic and copies ran while one was open for 0% of the time, Pallas kernels for 0%

commit v1 on v0

v1 whole, which is shorter than its diff:
```python
import functools

import jax
import jax.numpy as jnp
from jax import lax
from jax.experimental import pallas as pl
from jax.experimental.pallas import tpu as pltpu
from jax.sharding import PartitionSpec as P

F32, BF16 = jnp.float32, jnp.bfloat16
STEP = 0.15
HT, WD, C = 8, 16, 256
POS = HT * WD
TAPS = 9
NARROW = (False, True, True, True)


def kernel(ny, nz, nx, *refs):
    (x_ref, w_hbm, g_ref, ct_ref, st_ref, ad_ref, gr_ref) = refs[:7]
    (wf, wt, xch, cch, g2, gz, gy, buf, buf_s, u1s, u2s, dsc, at, atr, lhs, sg, gsend, grecv) = refs[7:25]
    snds, recvs, tots, sos, sts = (refs[25 + 4 * i : 29 + 4 * i] for i in range(5))
    (send_sem, recv_sem, w_sem) = refs[45:]

    depth, dp = lax.axis_index("depth"), lax.axis_index("dp")
    y, z = depth // nz, depth % nz
    xx, core = dp // 2, dp % 2
    rows = 2 * POS // nz
    per_half = nz // 2
    half = z // per_half
    cs = C // (2 * nx)

    def at_z(k):
        return (y * nz + k, dp)

    def at_y(k):
        return (k * nz + z, dp)

    def at_x(k):
        return (depth, k * 2 + core)

    sibling = (depth, xx * 2 + 1 - core)

    def over_z(body):
        def hop(i, _):
            body((z + nz // 2 + (1 - 2 * (i % 2)) * ((i + 1) // 2)) % nz)
            return 0

        lax.fori_loop(0, nz - 1, hop, 0)

    def over_y(body):
        for i in range(1, ny):
            body((y + i) % ny)

    def over_x(body):
        for i in range(1, nx):
            body((xx + i) % nx)

    def send(src, dst, index, device):
        pltpu.make_async_remote_copy(
            src_ref=src,
            dst_ref=dst,
            send_sem=send_sem.at[index],
            recv_sem=recv_sem.at[index],
            device_id=device,
            device_id_type=pl.DeviceIdType.MESH,
        ).start()

    def wait(ref, sem):
        pltpu.make_async_copy(ref, ref, sem).wait()

    barrier = pltpu.get_barrier_semaphore()

    def greet(device):
        pl.semaphore_signal(barrier, inc=1, device_id=device, device_id_type=pl.DeviceIdType.MESH)

    over_z(lambda k: greet(at_z(k)))
    over_y(lambda k: greet(at_y(k)))
    over_x(lambda k: greet(at_x(k)))
    greet(sibling)
    fetch = [pltpu.make_async_copy(w_hbm.at[i], wf.at[i], w_sem.at[i]) for i in range(2)]
    for copy in fetch:
        copy.start()

    gain = g_ref[...]
    for h in range(2):
        g2[h] = gain[:, 128 * h : 128 * h + 128]

    def chunked(dst, value):
        for k in range(nz):
            r, h = rows * (k % per_half), k // per_half
            dst[k] = value[r : r + rows, 128 * h : 128 * h + 128].astype(dst.dtype)

    x = x_ref[...].astype(F32)
    cot = ct_ref[...].astype(F32)
    chunked(xch, x)
    chunked(cch, cot)
    edge = jnp.zeros((WD, C), BF16)
    for b in (buf.at[0], buf.at[1], buf_s):
        for i in range(3):
            b[i, 0:WD] = edge
            b[i, POS + WD : POS + 2 * WD] = edge

    column = lax.broadcasted_iota(jnp.int32, (POS, C), 0) % WD

    def stage(b, value):
        b[0, WD : POS + WD] = jnp.where(column > 0, pltpu.roll(value, 1, 0), 0.0).astype(BF16)
        b[1, WD : POS + WD] = value.astype(BF16)
        b[2, WD : POS + WD] = jnp.where(column < WD - 1, pltpu.roll(value, POS - 1, 0), 0.0).astype(BF16)

    def conv(b, w, flip=False):
        total = None
        for t in range(TAPS):
            window = b[t % 3, WD * (t // 3) : WD * (t // 3) + POS]
            part = jnp.dot(window, w[8 - t if flip else t], preferred_element_type=F32)
            total = part if total is None else total + part
        return total

    def layer(b, u, w):
        stage(b, jnp.maximum(u, 0.0))
        return u + STEP * conv(b, w)

    def scan_order(reverse):
        return range(nz - 1, -1, -1) if reverse else range(nz)

    def offsets_out(p, offsets):
        chunked(snds[p], offsets)
        over_z(lambda k: send(snds[p].at[k], recvs[p].at[z], 3 * p, at_z(k)))
        recvs[p][z] = snds[p][z]

    def totals_out(p, reverse):
        wait(recvs[p].at[pl.ds(0, nz - 1)], recv_sem.at[3 * p])
        carry = None
        for k in scan_order(reverse):
            item = recvs[p][k].astype(F32)
            carry = item if carry is None else gz[k] * carry + item
        tots[p][y] = carry
        over_y(lambda k: send(tots[p].at[y], tots[p].at[y], 3 * p + 1, at_y(k)))

    def states_out(p, reverse, first):
        if ny > 1:
            wait(tots[p].at[pl.ds(0, ny - 1)], recv_sem.at[3 * p + 1])
        carry = first[z]
        for k in range(ny - 1, 0, -1) if reverse else range(ny - 1):
            reached = k > y if reverse else k < y
            carry = jnp.where(reached, gy[k] * carry + tots[p][k], carry)
        order = scan_order(reverse)
        for k in order:
            sos[p][k] = carry.astype(sos[p].dtype)
            if k != order[-1]:
                carry = gz[k] * carry + recvs[p][k].astype(F32)
        over_z(lambda k: send(sos[p].at[k], sts[p].at[z], 3 * p + 2, at_z(k)))
        sts[p][z] = sos[p][z]

    def states_in(p):
        wait(sts[p].at[pl.ds(0, nz - 1)], recv_sem.at[3 * p + 2])
        halves = []
        for h in range(2):
            halves.append(jnp.concatenate([sts[p][h * per_half + k] for k in range(per_half)], axis=0))
        return jnp.concatenate(halves, axis=1)

    fetch[0].wait()
    middle = layer(buf.at[0], x, wf.at[0])
    pl.semaphore_wait(barrier, (nz - 1) + (ny - 1) + (nx - 1) + 1)
    over_z(lambda k: send(g2.at[k // per_half], gz.at[z], 12, at_z(k)))
    gz[z] = g2[half]
    fetch[1].wait()
    final = layer(buf.at[1], middle, wf.at[1])
    offsets_out(0, final - gain * x)
    for i in range(2):

        def flip(t, _, i=i):
            wt[i, t] = wf[i, t].T
            return 0

        lax.fori_loop(0, TAPS, flip, 0)
    wait(gz.at[pl.ds(0, nz - 1)], recv_sem.at[12])
    product = gz[0]
    for k in range(1, nz):
        product = product * gz[k]
    gy[y] = product
    over_y(lambda k: send(gy.at[y], gy.at[y], 13, at_y(k)))
    totals_out(0, False)
    if ny > 1:
        wait(gy.at[pl.ds(0, ny - 1)], recv_sem.at[13])
    states_out(0, False, xch)
    u1 = states_in(0)

    def adjoint(e):
        stage(buf_s, (STEP * e).astype(BF16).astype(F32))
        e = e + jnp.where(u2s[...] > 0.0, conv(buf_s, wt.at[1], True), 0.0)
        stage(buf_s, (STEP * e).astype(BF16).astype(F32))
        return e + jnp.where(u1s[...] > 0.0, conv(buf_s, wt.at[0], True), 0.0)

    u1s[...] = u1
    u2s[...] = layer(buf.at[0], u1, wf.at[0])
    offsets_out(2, adjoint(cot) - gain * cot)
    u1, u2 = u1s[...], u2s[...]
    final = layer(buf.at[1], u2, wf.at[1])
    for i, u in enumerate((u1, u2)):
        turned = jnp.maximum(u, 0.0).T.astype(BF16)
        for k in range(nx):
            at[k, i] = turned[2 * cs * k : 2 * cs * (k + 1)]
    totals_out(2, True)
    over_x(lambda k: send(at.at[k], atr.at[xx], 14, at_x(k)))
    atr[xx] = at[xx]
    states_out(2, True, cch)
    chunked(snds[1], final - gain * u1)
    recvs[1][z] = snds[1][z]
    e1 = states_in(2).astype(F32)

    over_z(lambda k: send(snds[1].at[k], recvs[1].at[z], 3, at_z(k)))
    d = adjoint(e1) - gain * e1
    offsets_out(3, d)
    dsc[...] = d
    totals_out(1, False)
    wait(atr.at[pl.ds(0, nx - 1)], recv_sem.at[14])

    place = lax.broadcasted_iota(jnp.int32, (2 * cs, POS), 1)
    line, cell = place // WD, place % WD

    def windows(i, _):
        for k in range(nx):
            value = atr[k, i].astype(F32)
            for t in range(TAPS):
                down, right = t // 3 - 1, t % 3 - 1
                moved = value
                if t != 4:
                    ok = (line + down >= 0) & (line + down < HT) & (cell + right >= 0) & (cell + right < WD)
                    moved = jnp.where(ok, pltpu.roll(value, (-down * WD - right) % POS, 1), 0.0)
                moved = moved.astype(BF16)
                for c in range(2):
                    lhs[i, c, t, :, POS * k : POS * (k + 1)] = moved[cs * c : cs * (c + 1)]
        return 0

    lax.fori_loop(0, 2, windows, 0)
    totals_out(3, True)
    states_out(3, True, cch)
    e2 = states_in(3).astype(F32)

    def scaled_out(i, e):
        s = (STEP * e).astype(BF16)
        sg[i, xx] = s
        over_x(lambda k: send(sg.at[i, xx], sg.at[i, xx], 15 + i, at_x(k)))
        return s

    s = scaled_out(1, e2)
    stage(buf_s, s.astype(F32))
    scaled_out(0, e2 + jnp.where(u2s[...] > 0.0, conv(buf_s, wt.at[1], True), 0.0))
    states_out(1, False, xch)
    ad_ref[...] = (gain * e2 + dsc[...]).astype(BF16)

    def part(i, c):
        right = sg[i].reshape(nx * POS, C)
        return jnp.dot(lhs[i, c].reshape(TAPS * cs, nx * POS), right, preferred_element_type=F32)

    for i in (1, 0):
        wait(sg.at[i, pl.ds(0, nx - 1)], recv_sem.at[15 + i])
        gsend[i] = part(i, 1 - core).astype(BF16)
        send(gsend.at[i], grecv.at[i], 17 + i, sibling)
    mine = [part(i, core) for i in (0, 1)]
    st_ref[...] = states_in(1)
    for i in (1, 0):
        wait(grecv.at[i], recv_sem.at[17 + i])
        gr_ref[i] = (mine[i] + grecv[i].astype(F32)).astype(BF16)

    for p in range(4):
        wait(snds[p].at[pl.ds(0, nz - 1)], send_sem.at[3 * p])
        if ny > 1:
            wait(tots[p].at[pl.ds(0, ny - 1)], send_sem.at[3 * p + 1])
        wait(sos[p].at[pl.ds(0, nz - 1)], send_sem.at[3 * p + 2])
    wait(gz.at[pl.ds(0, nz - 1)], send_sem.at[12])
    if ny > 1:
        wait(gy.at[pl.ds(0, ny - 1)], send_sem.at[13])
    wait(atr.at[pl.ds(0, nx - 1)], send_sem.at[14])
    for i in range(2):
        wait(sg.at[i, pl.ds(0, nx - 1)], send_sem.at[15 + i])
        wait(grecv.at[i], send_sem.at[17 + i])


def program(mesh, ny, nz, nx):
    rows = 2 * POS // nz
    cs = C // (2 * nx)
    vmem = pltpu.VMEM
    widths = [BF16 if narrow else F32 for narrow in NARROW]
    scratch = [
        vmem((2, TAPS, C, C), BF16),
        vmem((2, TAPS, C, C), BF16),
        vmem((nz, rows, 128), F32),
        vmem((nz, rows, 128), F32),
        vmem((2, 1, 128), F32),
        vmem((nz, 1, 128), F32),
        vmem((ny, 1, 128), F32),
        vmem((2, 3, POS + 2 * WD, C), BF16),
        vmem((3, POS + 2 * WD, C), BF16),
        vmem((POS, C), F32),
        vmem((POS, C), F32),
        vmem((POS, C), F32),
        vmem((nx, 2, 2 * cs, POS), BF16),
        vmem((nx, 2, 2 * cs, POS), BF16),
        vmem((2, 2, TAPS, cs, nx * POS), BF16),
        vmem((2, nx, POS, C), BF16),
        vmem((2, TAPS * cs, C), BF16),
        vmem((2, TAPS * cs, C), BF16),
    ]
    chunks = [vmem((nz, rows, 128), width) for width in widths]
    scratch += chunks + chunks
    scratch += [vmem((ny, rows, 128), F32)] * 4
    scratch += chunks + chunks
    scratch += [pltpu.SemaphoreType.DMA((19,)), pltpu.SemaphoreType.DMA((19,)), pltpu.SemaphoreType.DMA((2,))]

    def per_device(features, weights, gains, cotangent):
        inside = pl.BlockSpec(memory_space=pltpu.VMEM)
        starts, adjoints, grads = pl.pallas_call(
            functools.partial(kernel, ny, nz, nx),
            out_shape=(
                jax.ShapeDtypeStruct((POS, C), BF16),
                jax.ShapeDtypeStruct((POS, C), BF16),
                jax.ShapeDtypeStruct((2, TAPS * cs, C), BF16),
            ),
            in_specs=[inside, pl.BlockSpec(memory_space=pl.ANY), inside, inside],
            out_specs=(inside, inside, inside),
            scratch_shapes=scratch,
            compiler_params=pltpu.CompilerParams(
                collective_id=0, has_side_effects=True, vmem_limit_bytes=48 * 1024 * 1024
            ),
        )(
            features.reshape(POS, C),
            weights.reshape(2, TAPS, C, C),
            gains,
            cotangent.reshape(POS, C),
        )
        return (
            starts.reshape(1, 1, HT, WD, C),
            adjoints.reshape(1, 1, HT, WD, C),
            grads.reshape(2, 3, 3, cs, C),
        )

    return jax.shard_map(
        per_device,
        mesh=mesh,
        in_specs=(
            P("dp", None, None, None),
            P("depth", None, None, None, None),
            P("depth", None),
            P("dp", None, None, None),
        ),
        out_specs=(
            P("depth", "dp", None, None, None),
            P("depth", "dp", None, None, None),
            P("depth", None, None, "dp", None),
        ),
        check_vma=False,
    )


def solution(mesh):
    return program(mesh, ny=4, nz=16, nx=4)
```

time: 1000 us -> 91.1 us (0.09)
  waiting for transfers between devices: 618 us -> 0 us
  other arithmetic: 266 us -> 0 us
  Pallas kernels: 0 us -> 84.2 us
  blocking collectives: 74.5 us -> 0 us
  between operations: 14.6 us -> 0.65 us
    all_gather x4 -> x0, waiting for transfers between devices: 535 us -> none  [prefix(): everything = jax.tree.map(lambda part: lax.all_gather(part, axis), value)]
    select_n x512 -> x0, other arithmetic: 257 us -> none  [hop(): return jax.tree.map(lambda a, b: jnp.where(reached, a, b), new, before)]
    pallas_call x0 -> x1, Pallas kernels: none -> 84.2 us  [per_device(): pl.pallas_call(functools.partial(kernel, ny, nz, nx), out_shape=(jax.Shap...]
    psum x1 -> x0, waiting for transfers between devices: 82.8 us -> none  [per_device(): summed = lax.psum(grads.astype(jnp.bfloat16), 'dp').astype(jnp.float32)]
    all_gather x1 -> x0, blocking collectives: 74.5 us -> none  [prefix(): everything = jax.tree.map(lambda part: lax.all_gather(part, axis), value)]
  transfers between devices with their start and end apart: 5 -> 0, of which waited for: 5 -> 0; matrix products, arithmetic and copies ran while one was open for 0% -> 0% of each run, Pallas kernels for 0% -> 0%
where the time goes in v1:
time: 91.1 us; the launch traced here: 90.8 us
  Pallas kernels  84.2 us (92%)
  local copies, waits for them, and re-layouts  5.99 us (7%)
    pallas_call x1, Pallas kernels, per_device(): pl.pallas_call(functools.partial(kernel, ny, nz, nx), out_shape=(jax.Shap...  84.2 us
    unnamed x11, local copies, waits for them, and re-layouts  5.99 us

profile of v1, /device:TPU:1, one launch (start us, length us, event | category | flops | bytes accessed | tf_op | source)
XLA Modules:
  0.0 90.8 jit_solution(5718120825627405105)
XLA Ops:
  0.6 0.0 copy-start
  0.6 1.7 %copy-done = bf16[2,3,3,256,256]{4,3,2,1,0:T(8,128)(2,1)S(1)} copy-done((bf16[2,3,3,256,256]{4,3,2,1,0:T(8,128)(2,1)S(1)}, bf16[2,3,3,256,256]{4,3,2,1,0:T(8,128)(2,1)}, u32[]{:S(2)}) %copy-start) | copy-done | bytes 2359320
  2.3 0.0 copy-start.1
  2.3 0.8 copy-done.1
  3.1 0.0 copy-start.2
  3.1 0.8 copy-done.2
  4.0 0.0 copy-start.3
  4.0 0.7 copy-done.3
  4.7 84.2 %shard_map.67 = (bf16[128,256]{1,0:T(8,128)(2,1)S(1)}, bf16[128,256]{1,0:T(8,128)(2,1)S(1)}, bf16[2,288,256]{2,1,0:T(8,128)(2,1)S(1)}) custom-call(bf16[128,256]{1,0:T(8,128)(2,1)S(1)} %bitcast.8, bf16[2,9,256,256]{3,2,1,0:T(8,128)(2,1)S(1)} %bitcast.6, f32[1,256]{1,0:T(1,128)S(1)} %copy-done.3, bf16[128,256]{1,0:T(8,128)(2,1)S(1)} %bitcast.9), custom_call_target="tpu_custom_call" | custom-call | tf_op jit(solution)/shard_map/pallas_call | solution.py:313
  88.9 0.6 copy.10
  89.5 0.6 copy.11
  90.1 0.7 copy.12
Async XLA Ops:
  0.6 1.7 %copy-start = (bf16[2,3,3,256,256]{4,3,2,1,0:T(8,128)(2,1)S(1)}, bf16[2,3,3,256,256]{4,3,2,1,0:T(8,128)(2,1)}, u32[]{:S(2)}) copy-start(bf16[2,3,3,256,256]{4,3,2,1,0:T(8,128)(2,1)} %param.5) | copy-start | bytes 7077892
  2.3 0.8 copy-start.1
  3.1 0.8 copy-start.2
  4.0 0.7 copy-start.3

commit v2 on v1

v2 whole, which is shorter than its diff:
```python
import functools

import jax
import jax.numpy as jnp
from jax import lax
from jax.experimental import pallas as pl
from jax.experimental.pallas import tpu as pltpu
from jax.sharding import PartitionSpec as P

F32, BF16 = jnp.float32, jnp.bfloat16
STEP = 0.15
HT, WD, C = 8, 16, 256
POS = HT * WD
TAPS = 9
VMEM_BYTES = 54000 * 1024
WIDTH = (F32, BF16, BF16, BF16)
OWNERS = (1, 1, 2, 2)


def kernel(ny, nz, nx, *refs):
    (x_hbm, w_hbm, g_hbm, ct_hbm, st_ref, ad_ref, gr_ref) = refs[:7]
    (x_ref, g_ref, ct_ref, wf, wt, xch, cch, g2, gz, gy) = refs[7:17]
    (buf, buf_s, u1s, u2s, dsc, at, atr, act, lhs, sg, s1g, gsend, grecv) = refs[17:30]
    snds, recvs, tots, sos, sts = (refs[30 + 4 * i : 34 + 4 * i] for i in range(5))
    (send_sem, recv_sem, fetch_sem) = refs[50:]

    depth, dp = lax.axis_index("depth"), lax.axis_index("dp")
    y, z = depth // nz, depth % nz
    xx, core = dp // 2, dp % 2
    chunks = [nz // m for m in OWNERS]
    mine = [z % n for n in chunks]
    half = [2 * mine[p] // chunks[p] for p in range(4)]
    cs = C // (2 * nx)

    def at_z(k):
        return (y * nz + k, dp)

    def at_y(k):
        return (k * nz + z, dp)

    def at_x(k):
        return (depth, k * 2 + core)

    sibling = (depth, xx * 2 + 1 - core)

    def over_z(body, n=nz):
        def hop(i, _):
            body((z + nz + (1 - 2 * (i % 2)) * (n // 2 - (i + 1) // 2)) % nz)
            return 0

        lax.fori_loop(0, n - 1, hop, 0)

    def over_y(body):
        for i in range(1, ny):
            body((y + i) % ny)

    def over_x(body):
        for i in sorted(range(1, nx), key=lambda i: -min(i, nx - i)):
            body(i, (xx + i) % nx)

    def send(src, dst, index, device):
        pltpu.make_async_remote_copy(
            src_ref=src,
            dst_ref=dst,
            send_sem=send_sem.at[index],
            recv_sem=recv_sem.at[index],
            device_id=device,
            device_id_type=pl.DeviceIdType.MESH,
        ).start()

    def wait(ref, sem):
        pltpu.make_async_copy(ref, ref, sem).wait()

    barrier = pltpu.get_barrier_semaphore()

    def greet(device):
        pl.semaphore_signal(barrier, inc=1, device_id=device, device_id_type=pl.DeviceIdType.MESH)

    over_z(lambda k: greet(at_z(k)))
    over_y(lambda k: greet(at_y(k)))
    over_x(lambda i, k: greet(at_x(k)))
    greet(sibling)
    pairs = [(x_hbm, x_ref), (w_hbm.at[0], wf.at[0]), (g_hbm, g_ref), (w_hbm.at[1], wf.at[1]), (ct_hbm, ct_ref)]
    fetch = [pltpu.make_async_copy(a, b, fetch_sem.at[i]) for i, (a, b) in enumerate(pairs)]
    for copy in fetch:
        copy.start()

    def chunked(dst, value):
        n, rows = dst.shape[0], dst.shape[1]
        for k in range(n):
            r, h = rows * (k % (n // 2)), 2 * k // n
            dst[k] = value[r : r + rows, 128 * h : 128 * h + 128].astype(dst.dtype)

    edge = jnp.zeros((WD, C), BF16)
    for b in (buf.at[0], buf.at[1], buf_s):
        for i in range(3):
            b[i, 0:WD] = edge
            b[i, POS + WD : POS + 2 * WD] = edge

    column = lax.broadcasted_iota(jnp.int32, (POS, C), 0) % WD

    def stage(b, value):
        b[0, WD : POS + WD] = jnp.where(column > 0, pltpu.roll(value, 1, 0), 0.0).astype(BF16)
        b[1, WD : POS + WD] = value.astype(BF16)
        b[2, WD : POS + WD] = jnp.where(column < WD - 1, pltpu.roll(value, POS - 1, 0), 0.0).astype(BF16)

    def conv(b, w, flip=False):
        total = None
        for t in range(TAPS):
            window = b[t % 3, WD * (t // 3) : WD * (t // 3) + POS]
            part = jnp.dot(window, w[8 - t if flip else t], preferred_element_type=F32)
            total = part if total is None else total + part
        return total

    def layer(b, u, w):
        stage(b, jnp.maximum(u, 0.0))
        return u + STEP * conv(b, w)

    def scan_order(reverse):
        return range(nz - 1, -1, -1) if reverse else range(nz)

    def offsets_out(p):
        over_z(lambda k: send(snds[p].at[k % chunks[p]], recvs[p].at[z], 3 * p, at_z(k)))

    def totals_out(p, reverse):
        wait(recvs[p].at[pl.ds(0, nz - 1)], recv_sem.at[3 * p])
        carry = None
        for k in scan_order(reverse):
            item = recvs[p][k].astype(F32)
            carry = item if carry is None else gz[k, half[p]] * carry + item
        tots[p][y] = carry
        over_y(lambda k: send(tots[p].at[y], tots[p].at[y], 3 * p + 1, at_y(k)))

    def states_out(p, reverse, first):
        if ny > 1:
            wait(tots[p].at[pl.ds(0, ny - 1)], recv_sem.at[3 * p + 1])
        carry = first[mine[p]]
        for k in range(ny - 1, 0, -1) if reverse else range(ny - 1):
            reached = k > y if reverse else k < y
            carry = jnp.where(reached, gy[k, half[p]] * carry + tots[p][k], carry)
        order = scan_order(reverse)
        for k in order:
            sos[p][k] = carry.astype(sos[p].dtype)
            if k != order[-1]:
                carry = gz[k, half[p]] * carry + recvs[p][k].astype(F32)
        over_z(lambda k: send(sos[p].at[k], sts[p].at[mine[p]], 3 * p + 2, at_z(k)), chunks[p])
        sts[p][mine[p]] = sos[p][z]

    def states_in(p):
        n = chunks[p]
        wait(sts[p].at[pl.ds(0, n - 1)], recv_sem.at[3 * p + 2])
        halves = []
        for h in range(2):
            halves.append(jnp.concatenate([sts[p][h * (n // 2) + k] for k in range(n // 2)], axis=0))
        return jnp.concatenate(halves, axis=1)

    fetch[0].wait()
    x = x_ref[...].astype(F32)
    fetch[1].wait()
    middle = layer(buf.at[0], x, wf.at[0])
    fetch[2].wait()
    gain = g_ref[...]
    for h in range(2):
        g2[h] = gain[:, 128 * h : 128 * h + 128]
    fetch[3].wait()
    chunked(snds[0], layer(buf.at[1], middle, wf.at[1]) - gain * x)
    pl.semaphore_wait(barrier, (nz - 1) + (ny - 1) + (nx - 1) + 1)
    offsets_out(0)
    over_z(lambda k: send(g2, gz.at[z], 12, at_z(k)))
    recvs[0][z] = snds[0][mine[0]]
    gz[z] = g2[...]
    fetch[4].wait()
    cot = ct_ref[...].astype(F32)
    chunked(xch, x)
    chunked(cch, cot)
    for i in range(2):

        def flip(t, _, i=i):
            wt[i, t] = wf[i, t].T
            return 0

        lax.fori_loop(0, TAPS, flip, 0)
    wait(gz.at[pl.ds(0, nz - 1)], recv_sem.at[12])
    product = gz[0]
    for k in range(1, nz):
        product = product * gz[k]
    gy[y] = product
    over_y(lambda k: send(gy.at[y], gy.at[y], 13, at_y(k)))
    totals_out(0, False)
    if ny > 1:
        wait(gy.at[pl.ds(0, ny - 1)], recv_sem.at[13])
    states_out(0, False, xch)
    u1 = states_in(0)

    def adjoint(e):
        stage(buf_s, (STEP * e).astype(BF16).astype(F32))
        e = e + jnp.where(u2s[...] > 0.0, conv(buf_s, wt.at[1], True), 0.0)
        stage(buf_s, (STEP * e).astype(BF16).astype(F32))
        return e + jnp.where(u1s[...] > 0.0, conv(buf_s, wt.at[0], True), 0.0)

    u1s[...] = u1
    u2s[...] = layer(buf.at[0], u1, wf.at[0])
    chunked(snds[2], adjoint(cot) - gain * cot)
    offsets_out(2)
    recvs[2][z] = snds[2][mine[2]]
    u1, u2 = u1s[...], u2s[...]
    for i, u in enumerate((u1, u2)):
        active = jnp.maximum(u, 0.0)
        turned = active.T.astype(BF16)
        for k in range(nx):
            at[k, i] = turned[2 * cs * k : 2 * cs * (k + 1)]
    act[xx] = active.astype(BF16)
    over_x(lambda i, k: send(at.at[k], atr.at[xx], 14, at_x(k)))
    over_x(lambda i, k: send(act.at[xx], act.at[xx], 15, at_x(k)))
    atr[xx] = at[xx]
    chunked(snds[1], layer(buf.at[1], u2, wf.at[1]) - gain * u1)
    totals_out(2, True)
    recvs[1][z] = snds[1][mine[1]]
    states_out(2, True, cch)
    offsets_out(1)
    e1 = states_in(2).astype(F32)

    d = adjoint(e1) - gain * e1
    chunked(snds[3], d)
    offsets_out(3)
    recvs[3][z] = snds[3][mine[3]]
    dsc[...] = d
    if nx > 1:
        wait(atr.at[pl.ds(0, nx - 1)], recv_sem.at[14])
        wait(act.at[pl.ds(0, nx - 1)], recv_sem.at[15])

    place = lax.broadcasted_iota(jnp.int32, (2 * cs, POS), 1)
    line, cell = place // WD, place % WD

    def windows(i, _):
        for k in range(nx):
            value = atr[k, i].astype(F32)
            for t in range(TAPS):
                down, right = t // 3 - 1, t % 3 - 1
                moved = value
                if t != 4:
                    ok = (line + down >= 0) & (line + down < HT) & (cell + right >= 0) & (cell + right < WD)
                    moved = jnp.where(ok, pltpu.roll(value, (-down * WD - right) % POS, 1), 0.0)
                moved = moved.astype(BF16)
                for c in range(2):
                    lhs[i, c, t, :, POS * k : POS * (k + 1)] = moved[cs * c : cs * (c + 1)]
        return 0

    lax.fori_loop(0, 2, windows, 0)
    totals_out(1, False)
    totals_out(3, True)
    states_out(3, True, cch)
    states_out(1, False, xch)
    e2 = states_in(3).astype(F32)

    s = (STEP * e2).astype(BF16)
    sg[xx] = s
    over_x(lambda i, k: send(sg.at[xx], sg.at[xx], 16 + i, at_x(k)))
    stage(buf_s, s.astype(F32))
    spread = conv(buf_s, wt.at[1], True)
    s1g[xx] = (STEP * (e2 + jnp.where(u2s[...] > 0.0, spread, 0.0))).astype(BF16)
    ad_ref[...] = (gain * e2 + dsc[...]).astype(BF16)

    def part(i, c, right):
        return jnp.dot(lhs[i, c].reshape(TAPS * cs, nx * POS), right[...].reshape(nx * POS, C), preferred_element_type=F32)

    def part_out(i, right):
        gsend[i] = part(i, 1 - core, right).astype(BF16)
        send(gsend.at[i], grecv.at[i], 16 + nx + i, sibling)

    arrivals = sorted(range(1, nx), key=lambda i: min(i, nx - i))
    for i in arrivals:
        k = (xx + nx - i) % nx
        wait(sg.at[0], recv_sem.at[16 + i])
        if i == arrivals[-1]:
            part_out(1, sg)
        s = sg[k].astype(F32)
        stage(buf_s, s)
        spread = conv(buf_s, wt.at[1], True)
        s1g[k] = (s + STEP * jnp.where(act[k].astype(F32) > 0.0, spread, 0.0)).astype(BF16)
    if nx == 1:
        part_out(1, sg)
    part_out(0, s1g)
    sums = [part(0, core, s1g), part(1, core, sg)]
    st_ref[...] = states_in(1)
    for i in (1, 0):
        wait(grecv.at[i], recv_sem.at[16 + nx + i])
        gr_ref[i] = (sums[i] + grecv[i].astype(F32)).astype(BF16)

    for p in range(4):
        wait(recvs[p].at[pl.ds(0, nz - 1)], send_sem.at[3 * p])
        if ny > 1:
            wait(tots[p].at[pl.ds(0, ny - 1)], send_sem.at[3 * p + 1])
        wait(sts[p].at[pl.ds(0, chunks[p] - 1)], send_sem.at[3 * p + 2])
    wait(gz.at[pl.ds(0, nz - 1)], send_sem.at[12])
    if ny > 1:
        wait(gy.at[pl.ds(0, ny - 1)], send_sem.at[13])
    if nx > 1:
        wait(atr.at[pl.ds(0, nx - 1)], send_sem.at[14])
        wait(act.at[pl.ds(0, nx - 1)], send_sem.at[15])
    for i in range(1, nx):
        wait(sg.at[0], send_sem.at[16 + i])
    for i in range(2):
        wait(grecv.at[i], send_sem.at[16 + nx + i])


def program(mesh, ny, nz, nx):
    cs = C // (2 * nx)
    vmem = pltpu.VMEM

    def states(m, width):
        return vmem((nz // m, 2 * POS * m // nz, 128), width)

    scratch = [
        vmem((POS, C), BF16),
        vmem((1, C), F32),
        vmem((POS, C), BF16),
        vmem((2, TAPS, C, C), BF16),
        vmem((2, TAPS, C, C), BF16),
        states(1, F32),
        states(2, F32),
        vmem((2, 1, 128), F32),
        vmem((nz, 2, 1, 128), F32),
        vmem((ny, 2, 1, 128), F32),
        vmem((2, 3, POS + 2 * WD, C), BF16),
        vmem((3, POS + 2 * WD, C), BF16),
        vmem((POS, C), F32),
        vmem((POS, C), F32),
        vmem((POS, C), F32),
        vmem((nx, 2, 2 * cs, POS), BF16),
        vmem((nx, 2, 2 * cs, POS), BF16),
        vmem((nx, POS, C), BF16),
        vmem((2, 2, TAPS, cs, nx * POS), BF16),
        vmem((nx, POS, C), BF16),
        vmem((nx, POS, C), BF16),
        vmem((2, TAPS * cs, C), BF16),
        vmem((2, TAPS * cs, C), BF16),
    ]
    kinds = list(zip(OWNERS, WIDTH))
    rows = [2 * POS * m // nz for m in OWNERS]
    scratch += [states(m, width) for m, width in kinds]
    scratch += [vmem((nz, r, 128), width) for r, width in zip(rows, WIDTH)]
    scratch += [vmem((ny, r, 128), F32) for r in rows]
    scratch += [vmem((nz, r, 128), width) for r, width in zip(rows, WIDTH)]
    scratch += [states(m, width) for m, width in kinds]
    sems = 18 + nx
    scratch += [pltpu.SemaphoreType.DMA((sems,)), pltpu.SemaphoreType.DMA((sems,)), pltpu.SemaphoreType.DMA((5,))]

    def per_device(features, weights, gains, cotangent):
        inside = pl.BlockSpec(memory_space=pltpu.VMEM)
        outside = pl.BlockSpec(memory_space=pltpu.HBM)
        shapes = (
            jax.ShapeDtypeStruct((POS, C), BF16),
            jax.ShapeDtypeStruct((POS, C), BF16),
            jax.ShapeDtypeStruct((2, TAPS * cs, C), BF16),
        )
        starts, adjoints, grads = pl.pallas_call(
            functools.partial(kernel, ny, nz, nx),
            out_shape=shapes,
            in_specs=[outside] * 4,
            out_specs=(inside,) * 3,
            scratch_shapes=scratch,
            compiler_params=pltpu.CompilerParams(
                collective_id=0, has_side_effects=True, vmem_limit_bytes=VMEM_BYTES
            ),
        )(
            features.reshape(POS, C),
            weights.reshape(2, TAPS, C, C),
            gains,
            cotangent.reshape(POS, C),
        )
        return (
            starts.reshape(1, 1, HT, WD, C),
            adjoints.reshape(1, 1, HT, WD, C),
            grads.reshape(2, 3, 3, cs, C),
        )

    return jax.shard_map(
        per_device,
        mesh=mesh,
        in_specs=(
            P("dp", None, None, None),
            P("depth", None, None, None, None),
            P("depth", None),
            P("dp", None, None, None),
        ),
        out_specs=(
            P("depth", "dp", None, None, None),
            P("depth", "dp", None, None, None),
            P("depth", None, None, "dp", None),
        ),
        check_vma=False,
    )


def solution(mesh):
    return program(mesh, ny=4, nz=16, nx=4)
```

time: 91.1 us -> 89.2 us (0.979)
  local copies, waits for them, and re-layouts: 5.99 us -> 4.32 us
    unnamed x11 -> x9, local copies, waits for them, and re-layouts: 5.99 us -> 4.32 us
where the time goes in v2:
time: 89.2 us; the launch traced here: 88.9 us
  Pallas kernels  83.9 us (94%)
  local copies, waits for them, and re-layouts  4.32 us (5%)
    pallas_call x1, Pallas kernels, per_device(): pl.pallas_call(functools.partial(kernel, ny, nz, nx), out_shape=shapes, i...  83.9 us
    unnamed x9, local copies, waits for them, and re-layouts  4.32 us

profile of v2, /device:TPU:1, one launch (start us, length us, event | category | flops | bytes accessed | tf_op | source)
XLA Modules:
  0.0 88.9 jit_solution(17298382050774454269)
XLA Ops:
  0.6 0.0 copy-start
  0.6 0.8 copy-done
  1.5 0.0 copy-start.1
  1.5 0.8 copy-done.1
  2.3 0.0 copy-start.2
  2.3 0.7 copy-done.2
  3.0 83.9 %shard_map.67 = (bf16[128,256]{1,0:T(8,128)(2,1)S(1)}, bf16[128,256]{1,0:T(8,128)(2,1)S(1)}, bf16[2,288,256]{2,1,0:T(8,128)(2,1)S(1)}) custom-call(bf16[128,256]{1,0:T(8,128)(2,1)S(1)} %bitcast.7, bf16[2,9,256,256]{3,2,1,0:T(8,128)(2,1)} %bitcast.11, f32[1,256]{1,0:T(1,128)S(1)} %copy-done.2, bf16[128,256]{1,0:T(8,128)(2,1)S(1)} %bitcast.8), custom_call_target="tpu_custom_call" | custom-call | tf_op jit(solution)/shard_map/pallas_call | solution.py:357
  86.9 0.6 copy.10
  87.6 0.6 copy.11
  88.2 0.7 copy.12
Async XLA Ops:
  0.6 0.8 copy-start
  1.5 0.8 copy-start.1
  2.3 0.7 copy-start.2

commit v3 on v2

--- a/solution.py
+++ b/solution.py
@@ -13,16 +13,16 @@
 POS = HT * WD
 TAPS = 9
 VMEM_BYTES = 54000 * 1024
-WIDTH = (F32, BF16, BF16, BF16)
-OWNERS = (1, 1, 2, 2)
+WIDTH = (BF16, BF16, BF16, BF16)
+OWNERS = (2, 1, 2, 2)
 
 
 def kernel(ny, nz, nx, *refs):
-    (x_hbm, w_hbm, g_hbm, ct_hbm, st_ref, ad_ref, gr_ref) = refs[:7]
-    (x_ref, g_ref, ct_ref, wf, wt, xch, cch, g2, gz, gy) = refs[7:17]
-    (buf, buf_s, u1s, u2s, dsc, at, atr, act, lhs, sg, s1g, gsend, grecv) = refs[17:30]
-    snds, recvs, tots, sos, sts = (refs[30 + 4 * i : 34 + 4 * i] for i in range(5))
-    (send_sem, recv_sem, fetch_sem) = refs[50:]
+    (in_ref, w_hbm, st_ref, ad_ref, gr_ref) = refs[:5]
+    (wf, wt, xch, xch2, cch, g2, gz, gy) = refs[5:13]
+    (buf, buf_s, u1s, u2s, dsc, at, atr, act, lhs, sg, s1g, gsend, grecv) = refs[13:26]
+    snds, recvs, tots, sos, sts = (refs[26 + 4 * i : 30 + 4 * i] for i in range(5))
+    (send_sem, recv_sem, fetch_sem) = refs[46:]
 
     depth, dp = lax.axis_index("depth"), lax.axis_index("dp")
     y, z = depth // nz, depth % nz
@@ -41,6 +41,8 @@
     def at_x(k):
         return (depth, k * 2 + core)
 
+    arrivals = sorted(range(1, nx), key=lambda i: min(i, nx - i))
+    slot = {i: n + 1 for n, i in enumerate(arrivals)}
     sibling = (depth, xx * 2 + 1 - core)
 
     def over_z(body, n=nz):
@@ -55,7 +57,7 @@
             body((y + i) % ny)
 
     def over_x(body):
-        for i in sorted(range(1, nx), key=lambda i: -min(i, nx - i)):
+        for i in reversed(arrivals):
             body(i, (xx + i) % nx)
 
     def send(src, dst, index, device):
@@ -80,8 +82,7 @@
     over_y(lambda k: greet(at_y(k)))
     over_x(lambda i, k: greet(at_x(k)))
     greet(sibling)
-    pairs = [(x_hbm, x_ref), (w_hbm.at[0], wf.at[0]), (g_hbm, g_ref), (w_hbm.at[1], wf.at[1]), (ct_hbm, ct_ref)]
-    fetch = [pltpu.make_async_copy(a, b, fetch_sem.at[i]) for i, (a, b) in enumerate(pairs)]
+    fetch = [pltpu.make_async_copy(w_hbm.at[i], wf.at[i], fetch_sem.at[i]) for i in range(2)]
     for copy in fetch:
         copy.start()
 
@@ -154,24 +155,22 @@
             halves.append(jnp.concatenate([sts[p][h * (n // 2) + k] for k in range(n // 2)], axis=0))
         return jnp.concatenate(halves, axis=1)
 
+    x = in_ref[0:POS]
+    cot = in_ref[POS : 2 * POS]
+    gain = in_ref[2 * POS : 2 * POS + 1]
     fetch[0].wait()
-    x = x_ref[...].astype(F32)
-    fetch[1].wait()
     middle = layer(buf.at[0], x, wf.at[0])
-    fetch[2].wait()
-    gain = g_ref[...]
     for h in range(2):
         g2[h] = gain[:, 128 * h : 128 * h + 128]
-    fetch[3].wait()
+    fetch[1].wait()
     chunked(snds[0], layer(buf.at[1], middle, wf.at[1]) - gain * x)
     pl.semaphore_wait(barrier, (nz - 1) + (ny - 1) + (nx - 1) + 1)
     offsets_out(0)
     over_z(lambda k: send(g2, gz.at[z], 12, at_z(k)))
     recvs[0][z] = snds[0][mine[0]]
     gz[z] = g2[...]
-    fetch[4].wait()
-    cot = ct_ref[...].astype(F32)
     chunked(xch, x)
+    chunked(xch2, x)
     chunked(cch, cot)
     for i in range(2):
 
@@ -189,8 +188,8 @@
     totals_out(0, False)
     if ny > 1:
         wait(gy.at[pl.ds(0, ny - 1)], recv_sem.at[13])
-    states_out(0, False, xch)
-    u1 = states_in(0)
+    states_out(0, False, xch2)
+    u1 = states_in(0).astype(F32)
 
     def adjoint(e):
         stage(buf_s, (STEP * e).astype(BF16).astype(F32))
@@ -209,10 +208,10 @@
         turned = active.T.astype(BF16)
         for k in range(nx):
             at[k, i] = turned[2 * cs * k : 2 * cs * (k + 1)]
-    act[xx] = active.astype(BF16)
-    over_x(lambda i, k: send(at.at[k], atr.at[xx], 14, at_x(k)))
-    over_x(lambda i, k: send(act.at[xx], act.at[xx], 15, at_x(k)))
-    atr[xx] = at[xx]
+    act[0] = active.astype(BF16)
+    over_x(lambda i, k: send(at.at[k], atr.at[slot[i]], 14, at_x(k)))
+    over_x(lambda i, k: send(act.at[0], act.at[slot[i]], 15, at_x(k)))
+    atr[0] = at[xx]
     chunked(snds[1], layer(buf.at[1], u2, wf.at[1]) - gain * u1)
     totals_out(2, True)
     recvs[1][z] = snds[1][mine[1]]
@@ -254,34 +253,38 @@
     e2 = states_in(3).astype(F32)
 
     s = (STEP * e2).astype(BF16)
-    sg[xx] = s
-    over_x(lambda i, k: send(sg.at[xx], sg.at[xx], 16 + i, at_x(k)))
+    sg[0] = s
+    over_x(lambda i, k: send(sg.at[0], sg.at[slot[i]], 16 + i, at_x(k)))
     stage(buf_s, s.astype(F32))
     spread = conv(buf_s, wt.at[1], True)
-    s1g[xx] = (STEP * (e2 + jnp.where(u2s[...] > 0.0, spread, 0.0))).astype(BF16)
+    s1g[0] = (STEP * (e2 + jnp.where(u2s[...] > 0.0, spread, 0.0))).astype(BF16)
     ad_ref[...] = (gain * e2 + dsc[...]).astype(BF16)
 
-    def part(i, c, right):
-        return jnp.dot(lhs[i, c].reshape(TAPS * cs, nx * POS), right[...].reshape(nx * POS, C), preferred_element_type=F32)
-
-    def part_out(i, right):
-        gsend[i] = part(i, 1 - core, right).astype(BF16)
-        send(gsend.at[i], grecv.at[i], 16 + nx + i, sibling)
-
-    arrivals = sorted(range(1, nx), key=lambda i: min(i, nx - i))
-    for i in arrivals:
-        k = (xx + nx - i) % nx
-        wait(sg.at[0], recv_sem.at[16 + i])
-        if i == arrivals[-1]:
-            part_out(1, sg)
-        s = sg[k].astype(F32)
+    def part(i, c, first, last):
+        count = last - first
+        left = lhs[i, c, :, :, first * POS : last * POS].reshape(TAPS * cs, count * POS)
+        right = (s1g, sg)[i][first:last].reshape(count * POS, C)
+        return jnp.dot(left, right, preferred_element_type=F32)
+
+    def below(i):
+        s = sg[slot[i]].astype(F32)
         stage(buf_s, s)
         spread = conv(buf_s, wt.at[1], True)
-        s1g[k] = (s + STEP * jnp.where(act[k].astype(F32) > 0.0, spread, 0.0)).astype(BF16)
-    if nx == 1:
-        part_out(1, sg)
-    part_out(0, s1g)
-    sums = [part(0, core, s1g), part(1, core, sg)]
+        s1g[slot[i]] = (s + STEP * jnp.where(act[slot[i]].astype(F32) > 0.0, spread, 0.0)).astype(BF16)
+
+    for i in arrivals[:-1]:
+        wait(sg.at[0], recv_sem.at[16 + i])
+        below(i)
+    cores = (1 - core, core)
+    early = [[part(i, c, 0, nx - 1) for c in cores] for i in range(2)]
+    wait(sg.at[0], recv_sem.at[16 + arrivals[-1]])
+    sums = [None, None]
+    for i in (1, 0):
+        if i == 0:
+            below(arrivals[-1])
+        gsend[i] = (early[i][0] + part(i, cores[0], nx - 1, nx)).astype(BF16)
+        send(gsend.at[i], grecv.at[i], 16 + nx + i, sibling)
+        sums[i] = early[i][1] + part(i, cores[1], nx - 1, nx)
     st_ref[...] = states_in(1)
     for i in (1, 0):
         wait(grecv.at[i], recv_sem.at[16 + nx + i])
@@ -312,12 +315,10 @@
         return vmem((nz // m, 2 * POS * m // nz, 128), width)
 
     scratch = [
-        vmem((POS, C), BF16),
-        vmem((1, C), F32),
-        vmem((POS, C), BF16),
         vmem((2, TAPS, C, C), BF16),
         vmem((2, TAPS, C, C), BF16),
         states(1, F32),
+        states(2, F32),
         states(2, F32),
         vmem((2, 1, 128), F32),
         vmem((nz, 2, 1, 128), F32),
@@ -344,7 +345,7 @@
     scratch += [vmem((nz, r, 128), width) for r, width in zip(rows, WIDTH)]
     scratch += [states(m, width) for m, width in kinds]
     sems = 18 + nx
-    scratch += [pltpu.SemaphoreType.DMA((sems,)), pltpu.SemaphoreType.DMA((sems,)), pltpu.SemaphoreType.DMA((5,))]
+    scratch += [pltpu.SemaphoreType.DMA((sems,)), pltpu.SemaphoreType.DMA((sems,)), pltpu.SemaphoreType.DMA((2,))]
 
     def per_device(features, weights, gains, cotangent):
         inside = pl.BlockSpec(memory_space=pltpu.VMEM)
@@ -354,20 +355,25 @@
             jax.ShapeDtypeStruct((POS, C), BF16),
             jax.ShapeDtypeStruct((2, TAPS * cs, C), BF16),
         )
+        packed = jnp.concatenate(
+            [
+                features.reshape(POS, C).astype(F32),
+                cotangent.reshape(POS, C).astype(F32),
+                jnp.broadcast_to(gains, (8, C)),
+            ]
+        )
         starts, adjoints, grads = pl.pallas_call(
             functools.partial(kernel, ny, nz, nx),
             out_shape=shapes,
-            in_specs=[outside] * 4,
+            in_specs=[inside, outside],
             out_specs=(inside,) * 3,
             scratch_shapes=scratch,
             compiler_params=pltpu.CompilerParams(
                 collective_id=0, has_side_effects=True, vmem_limit_bytes=VMEM_BYTES
             ),
         )(
-            features.reshape(POS, C),
+            packed,
             weights.reshape(2, TAPS, C, C),
-            gains,
-            cotangent.reshape(POS, C),
         )
         return (
             starts.reshape(1, 1, HT, WD, C),

time: 89.2 us -> 85 us (0.953)
  Pallas kernels: 83.9 us -> 80.6 us
  local copies, waits for them, and re-layouts: 4.32 us -> 2.66 us
  other arithmetic: 0 us -> 0.91 us
    pallas_call x1, Pallas kernels: 83.9 us -> 80.6 us  [per_device(): pl.pallas_call(functools.partial(kernel, ny, nz, nx), out_shape=shapes, i...]
    unnamed x9 -> x3, local copies, waits for them, and re-layouts: 4.32 us -> 1.97 us
where the time goes in v3:
time: 85 us; the launch traced here: 84.8 us
  Pallas kernels  80.6 us (95%)
  local copies, waits for them, and re-layouts  2.66 us (3%)
  other arithmetic  0.91 us (1%)
    pallas_call x1, Pallas kernels, per_device(): pl.pallas_call(functools.partial(kernel, ny, nz, nx), out_shape=shapes, i...  80.6 us
    unnamed x3, local copies, waits for them, and re-layouts  1.97 us

profile of v3, /device:TPU:1, one launch (start us, length us, event | category | flops | bytes accessed | tf_op | source)
XLA Modules:
  0.0 84.8 jit_solution(9420429225724548173)
XLA Ops:
  0.6 0.7 broadcast_in_dim.8
  1.3 0.9 %bitcast_convert_fusion = (f32[128,256]{1,0:T(8,128)S(1)}, f32[128,256]{1,0:T(8,128)S(1)}) fusion(bf16[1,8,16,256]{3,2,1,0:T(8,128)(2,1)} %param.7, bf16[1,8,16,256]{3,2,1,0:T(8,128)(2,1)} %param.4), kind=kLoop, calls=%fused_computation.1 | loop fusion | flops 65536 | bytes 393216 | tf_op jit(solution)/shard_map/convert_element_type | solution.py:361
  2.2 80.6 %shard_map.67 = (bf16[128,256]{1,0:T(8,128)(2,1)S(1)}, bf16[128,256]{1,0:T(8,128)(2,1)S(1)}, bf16[2,288,256]{2,1,0:T(8,128)(2,1)S(1)}) custom-call(f32[264,256]{1,0:T(8,128)S(1)} %pad_maximum_fusion.refs_0_, bf16[2,9,256,256]{3,2,1,0:T(8,128)(2,1)} %bitcast.14), custom_call_target="tpu_custom_call" | custom-call | tf_op jit(solution)/shard_map/pallas_call | solution.py:365
  82.8 0.6 copy.10
  83.5 0.6 copy.11
  84.1 0.7 copy.12
  (1 shorter events, 0.0 us)

commit v4 on v3

--- a/solution.py
+++ b/solution.py
@@ -20,7 +20,7 @@
 def kernel(ny, nz, nx, *refs):
     (in_ref, w_hbm, st_ref, ad_ref, gr_ref) = refs[:5]
     (wf, wt, xch, xch2, cch, g2, gz, gy) = refs[5:13]
-    (buf, buf_s, u1s, u2s, dsc, at, atr, act, lhs, sg, s1g, gsend, grecv) = refs[13:26]
+    (buf, buf_s, us, es, dsc, at, atr, act, lhs, sg, gsend, grecv, sums) = refs[13:26]
     snds, recvs, tots, sos, sts = (refs[26 + 4 * i : 30 + 4 * i] for i in range(5))
     (send_sem, recv_sem, fetch_sem) = refs[46:]
 
@@ -129,7 +129,7 @@
         for k in scan_order(reverse):
             item = recvs[p][k].astype(F32)
             carry = item if carry is None else gz[k, half[p]] * carry + item
-        tots[p][y] = carry
+        tots[p][y] = carry.astype(tots[p].dtype)
         over_y(lambda k: send(tots[p].at[y], tots[p].at[y], 3 * p + 1, at_y(k)))
 
     def states_out(p, reverse, first):
@@ -138,7 +138,7 @@
         carry = first[mine[p]]
         for k in range(ny - 1, 0, -1) if reverse else range(ny - 1):
             reached = k > y if reverse else k < y
-            carry = jnp.where(reached, gy[k, half[p]] * carry + tots[p][k], carry)
+            carry = jnp.where(reached, gy[k, half[p]] * carry + tots[p][k].astype(F32), carry)
         order = scan_order(reverse)
         for k in order:
             sos[p][k] = carry.astype(sos[p].dtype)
@@ -192,17 +192,23 @@
     u1 = states_in(0).astype(F32)
 
     def adjoint(e):
-        stage(buf_s, (STEP * e).astype(BF16).astype(F32))
-        e = e + jnp.where(u2s[...] > 0.0, conv(buf_s, wt.at[1], True), 0.0)
-        stage(buf_s, (STEP * e).astype(BF16).astype(F32))
-        return e + jnp.where(u1s[...] > 0.0, conv(buf_s, wt.at[0], True), 0.0)
-
-    u1s[...] = u1
-    u2s[...] = layer(buf.at[0], u1, wf.at[0])
+        es[...] = e
+
+        def one(n, _):
+            stage(buf_s, (STEP * es[...]).astype(BF16).astype(F32))
+            spread = conv(buf_s, wt.at[1 - n], True)
+            es[...] = es[...] + jnp.where(us[1 - n] > 0.0, spread, 0.0)
+            return 0
+
+        lax.fori_loop(0, 2, one, 0)
+        return es[...]
+
+    us[0] = u1
+    us[1] = layer(buf.at[0], u1, wf.at[0])
     chunked(snds[2], adjoint(cot) - gain * cot)
     offsets_out(2)
     recvs[2][z] = snds[2][mine[2]]
-    u1, u2 = u1s[...], u2s[...]
+    u1, u2 = us[0], us[1]
     for i, u in enumerate((u1, u2)):
         active = jnp.maximum(u, 0.0)
         turned = active.T.astype(BF16)
@@ -231,21 +237,22 @@
     place = lax.broadcasted_iota(jnp.int32, (2 * cs, POS), 1)
     line, cell = place // WD, place % WD
 
-    def windows(i, _):
-        for k in range(nx):
-            value = atr[k, i].astype(F32)
-            for t in range(TAPS):
-                down, right = t // 3 - 1, t % 3 - 1
-                moved = value
-                if t != 4:
-                    ok = (line + down >= 0) & (line + down < HT) & (cell + right >= 0) & (cell + right < WD)
-                    moved = jnp.where(ok, pltpu.roll(value, (-down * WD - right) % POS, 1), 0.0)
-                moved = moved.astype(BF16)
-                for c in range(2):
-                    lhs[i, c, t, :, POS * k : POS * (k + 1)] = moved[cs * c : cs * (c + 1)]
+    def windows(n, _):
+        i, k = n // nx, n % nx
+        value = atr[k, i].astype(F32)
+        lanes = pl.ds(pl.multiple_of(POS * k, POS), POS)
+        for t in range(TAPS):
+            down, right = t // 3 - 1, t % 3 - 1
+            moved = value
+            if t != 4:
+                ok = (line + down >= 0) & (line + down < HT) & (cell + right >= 0) & (cell + right < WD)
+                moved = jnp.where(ok, pltpu.roll(value, (-down * WD - right) % POS, 1), 0.0)
+            moved = moved.astype(BF16)
+            for c in range(2):
+                lhs[i, c, t, :, lanes] = moved[cs * c : cs * (c + 1)]
         return 0
 
-    lax.fori_loop(0, 2, windows, 0)
+    lax.fori_loop(0, 2 * nx, windows, 0)
     totals_out(1, False)
     totals_out(3, True)
     states_out(3, True, cch)
@@ -253,40 +260,40 @@
     e2 = states_in(3).astype(F32)
 
     s = (STEP * e2).astype(BF16)
-    sg[0] = s
-    over_x(lambda i, k: send(sg.at[0], sg.at[slot[i]], 16 + i, at_x(k)))
-    stage(buf_s, s.astype(F32))
-    spread = conv(buf_s, wt.at[1], True)
-    s1g[0] = (STEP * (e2 + jnp.where(u2s[...] > 0.0, spread, 0.0))).astype(BF16)
-    ad_ref[...] = (gain * e2 + dsc[...]).astype(BF16)
-
-    def part(i, c, first, last):
-        count = last - first
-        left = lhs[i, c, :, :, first * POS : last * POS].reshape(TAPS * cs, count * POS)
-        right = (s1g, sg)[i][first:last].reshape(count * POS, C)
-        return jnp.dot(left, right, preferred_element_type=F32)
-
-    def below(i):
-        s = sg[slot[i]].astype(F32)
+    sg[1, 0] = s
+    over_x(lambda i, k: send(sg.at[1, 0], sg.at[1, slot[i]], 16 + slot[i], at_x(k)))
+
+    def below(n, _):
+        @pl.when(n > 0)
+        def _():
+            wait(sg.at[1, 0], recv_sem.at[16 + n])
+
+        s = sg[1, n].astype(F32)
         stage(buf_s, s)
         spread = conv(buf_s, wt.at[1], True)
-        s1g[slot[i]] = (s + STEP * jnp.where(act[slot[i]].astype(F32) > 0.0, spread, 0.0)).astype(BF16)
-
-    for i in arrivals[:-1]:
-        wait(sg.at[0], recv_sem.at[16 + i])
-        below(i)
-    cores = (1 - core, core)
-    early = [[part(i, c, 0, nx - 1) for c in cores] for i in range(2)]
-    wait(sg.at[0], recv_sem.at[16 + arrivals[-1]])
-    sums = [None, None]
-    for i in (1, 0):
-        if i == 0:
-            below(arrivals[-1])
-        gsend[i] = (early[i][0] + part(i, cores[0], nx - 1, nx)).astype(BF16)
+        sg[0, n] = (s + STEP * jnp.where(act[n].astype(F32) > 0.0, spread, 0.0)).astype(BF16)
+
+        @pl.when(n == 0)
+        def _():
+            ad_ref[...] = (gain * e2 + dsc[...]).astype(BF16)
+
+        return 0
+
+    lax.fori_loop(0, nx, below, 0)
+
+    def part(i, c):
+        left = lhs[i, c].reshape(TAPS * cs, nx * POS)
+        return jnp.dot(left, sg[i].reshape(nx * POS, C), preferred_element_type=F32)
+
+    def parts(i, _):
+        gsend[i] = part(i, 1 - core).astype(BF16)
         send(gsend.at[i], grecv.at[i], 16 + nx + i, sibling)
-        sums[i] = early[i][1] + part(i, cores[1], nx - 1, nx)
+        sums[i] = part(i, core)
+        return 0
+
+    lax.fori_loop(0, 2, parts, 0)
     st_ref[...] = states_in(1)
-    for i in (1, 0):
+    for i in range(2):
         wait(grecv.at[i], recv_sem.at[16 + nx + i])
         gr_ref[i] = (sums[i] + grecv[i].astype(F32)).astype(BF16)
 
@@ -302,7 +309,7 @@
         wait(atr.at[pl.ds(0, nx - 1)], send_sem.at[14])
         wait(act.at[pl.ds(0, nx - 1)], send_sem.at[15])
     for i in range(1, nx):
-        wait(sg.at[0], send_sem.at[16 + i])
+        wait(sg.at[1, 0], send_sem.at[16 + i])
     for i in range(2):
         wait(grecv.at[i], send_sem.at[16 + nx + i])
 
@@ -325,25 +332,26 @@
         vmem((ny, 2, 1, 128), F32),
         vmem((2, 3, POS + 2 * WD, C), BF16),
         vmem((3, POS + 2 * WD, C), BF16),
-        vmem((POS, C), F32),
+        vmem((2, POS, C), F32),
         vmem((POS, C), F32),
         vmem((POS, C), F32),
         vmem((nx, 2, 2 * cs, POS), BF16),
         vmem((nx, 2, 2 * cs, POS), BF16),
         vmem((nx, POS, C), BF16),
         vmem((2, 2, TAPS, cs, nx * POS), BF16),
-        vmem((nx, POS, C), BF16),
-        vmem((nx, POS, C), BF16),
+        vmem((2, nx, POS, C), BF16),
         vmem((2, TAPS * cs, C), BF16),
         vmem((2, TAPS * cs, C), BF16),
+        vmem((2, TAPS * cs, C), F32),
     ]
     kinds = list(zip(OWNERS, WIDTH))
     rows = [2 * POS * m // nz for m in OWNERS]
     scratch += [states(m, width) for m, width in kinds]
     scratch += [vmem((nz, r, 128), width) for r, width in zip(rows, WIDTH)]
-    scratch += [vmem((ny, r, 128), F32) for r in rows]
-    scratch += [vmem((nz, r, 128), width) for r, width in zip(rows, WIDTH)]
-    scratch += [states(m, width) for m, width in kinds]
+    scratch += [vmem((ny, r, 128), width) for r, width in zip(rows, (F32, BF16, BF16, BF16))]
+    back = (F32, BF16, BF16, BF16)
+    scratch += [vmem((nz, r, 128), width) for r, width in zip(rows, back)]
+    scratch += [states(m, width) for m, width in zip(OWNERS, back)]
     sems = 18 + nx
     scratch += [pltpu.SemaphoreType.DMA((sems,)), pltpu.SemaphoreType.DMA((sems,)), pltpu.SemaphoreType.DMA((2,))]
 

time: 85 us -> 85 us (level)
  no operation moved by 1% of the time
where the time goes in v4:
time: 85 us; the launch traced here: 84.8 us
  Pallas kernels  80.6 us (95%)
  local copies, waits for them, and re-layouts  2.66 us (3%)
  other arithmetic  0.91 us (1%)
    pallas_call x1, Pallas kernels, per_device(): pl.pallas_call(functools.partial(kernel, ny, nz, nx), out_shape=shapes, i...  80.6 us
    unnamed x3, local copies, waits for them, and re-layouts  1.97 us

profile of v4, /device:TPU:1, one launch (start us, length us, event | category | flops | bytes accessed | tf_op | source)
XLA Modules:
  0.0 84.8 jit_solution(15508437803681314158)
XLA Ops:
  0.6 0.7 broadcast_in_dim.8
  1.3 0.9 %bitcast_convert_fusion = (f32[128,256]{1,0:T(8,128)S(1)}, f32[128,256]{1,0:T(8,128)S(1)}) fusion(bf16[1,8,16,256]{3,2,1,0:T(8,128)(2,1)} %param.7, bf16[1,8,16,256]{3,2,1,0:T(8,128)(2,1)} %param.4), kind=kLoop, calls=%fused_computation.1 | loop fusion | flops 65536 | bytes 393216 | tf_op jit(solution)/shard_map/convert_element_type | solution.py:369
  2.2 80.6 %shard_map.67 = (bf16[128,256]{1,0:T(8,128)(2,1)S(1)}, bf16[128,256]{1,0:T(8,128)(2,1)S(1)}, bf16[2,288,256]{2,1,0:T(8,128)(2,1)S(1)}) custom-call(f32[264,256]{1,0:T(8,128)S(1)} %pad_maximum_fusion.refs_0_, bf16[2,9,256,256]{3,2,1,0:T(8,128)(2,1)} %bitcast.14), custom_call_target="tpu_custom_call" | custom-call | tf_op jit(solution)/shard_map/pallas_call | solution.py:373
  82.8 0.6 copy.10
  83.5 0.6 copy.11
  84.1 0.7 copy.12
  (1 shorter events, 0.0 us)

commit v5 on v4

--- a/solution.py
+++ b/solution.py
@@ -19,7 +19,7 @@
 
 def kernel(ny, nz, nx, *refs):
     (in_ref, w_hbm, st_ref, ad_ref, gr_ref) = refs[:5]
-    (wf, wt, xch, xch2, cch, g2, gz, gy) = refs[5:13]
+    (wf, wt, xch, zeros, cch, g2, gz, gy) = refs[5:13]
     (buf, buf_s, us, es, dsc, at, atr, act, lhs, sg, gsend, grecv, sums) = refs[13:26]
     snds, recvs, tots, sos, sts = (refs[26 + 4 * i : 30 + 4 * i] for i in range(5))
     (send_sem, recv_sem, fetch_sem) = refs[46:]
@@ -170,7 +170,7 @@
     recvs[0][z] = snds[0][mine[0]]
     gz[z] = g2[...]
     chunked(xch, x)
-    chunked(xch2, x)
+    zeros[...] = jnp.zeros_like(zeros)
     chunked(cch, cot)
     for i in range(2):
 
@@ -188,8 +188,14 @@
     totals_out(0, False)
     if ny > 1:
         wait(gy.at[pl.ds(0, ny - 1)], recv_sem.at[13])
-    states_out(0, False, xch2)
-    u1 = states_in(0).astype(F32)
+    states_out(0, False, zeros)
+    factor = jnp.ones((2, 1, 128), F32)
+    for k in range(ny - 1):
+        factor = jnp.where(k < y, factor * gy[k], factor)
+    for k in range(nz - 1):
+        factor = jnp.where(k < z, factor * gz[k], factor)
+    factor = jnp.concatenate([factor[0], factor[1]], axis=1)
+    u1 = states_in(0).astype(F32) + factor * x
 
     def adjoint(e):
         es[...] = e

time: 85 us -> 85.2 us (level)
  no operation moved by 1% of the time
where the time goes in v5:
time: 85.2 us; the launch traced here: 84.9 us
  Pallas kernels  80.7 us (95%)
  local copies, waits for them, and re-layouts  2.66 us (3%)
  other arithmetic  0.91 us (1%)
    pallas_call x1, Pallas kernels, per_device(): pl.pallas_call(functools.partial(kernel, ny, nz, nx), out_shape=shapes, i...  80.7 us
    unnamed x3, local copies, waits for them, and re-layouts  1.97 us

profile of v5, /device:TPU:1, one launch (start us, length us, event | category | flops | bytes accessed | tf_op | source)
XLA Modules:
  0.0 84.9 jit_solution(1886212447523823461)
XLA Ops:
  0.6 0.7 broadcast_in_dim.8
  1.3 0.9 %bitcast_convert_fusion = (f32[128,256]{1,0:T(8,128)S(1)}, f32[128,256]{1,0:T(8,128)S(1)}) fusion(bf16[1,8,16,256]{3,2,1,0:T(8,128)(2,1)} %param.7, bf16[1,8,16,256]{3,2,1,0:T(8,128)(2,1)} %param.4), kind=kLoop, calls=%fused_computation.1 | loop fusion | flops 65536 | bytes 393216 | tf_op jit(solution)/shard_map/convert_element_type | solution.py:375
  2.2 80.7 %shard_map.67 = (bf16[128,256]{1,0:T(8,128)(2,1)S(1)}, bf16[128,256]{1,0:T(8,128)(2,1)S(1)}, bf16[2,288,256]{2,1,0:T(8,128)(2,1)S(1)}) custom-call(f32[264,256]{1,0:T(8,128)S(1)} %pad_maximum_fusion.refs_0_, bf16[2,9,256,256]{3,2,1,0:T(8,128)(2,1)} %bitcast.14), custom_call_target="tpu_custom_call" | custom-call | tf_op jit(solution)/shard_map/pallas_call | solution.py:379
  83.0 0.6 copy.10
  83.6 0.6 copy.11
  84.2 0.7 copy.12
  (1 shorter events, 0.0 us)
